TPU v7x, 32 devices: a whole 2x2x4 slice. The times are simulated.
32 devices in a mesh: grp: 2 (over x), tm: 16 (over z, y, core).
Axes of the slice: x: 2, y: 2, z: 4, core: 2. Of those that a mesh axis runs over, the one named last changes fastest.
Arguments:
- right_sides: float32 [64, 4, 128], P(('grp', 'tm')), parts along dimension 0, may hold values from -6 to 6
- obs_var: float32 [64, 128], P(('grp', 'tm')), parts along dimension 0, may hold values from 0.25 to 1
- footprint: bfloat16 [512, 8, 128, 128], P(('grp', 'tm')), parts along dimension 0, may hold values from -0.5 to 0.5
- tile_block: int32 [512, 8], P(('grp', 'tm')), parts along dimension 0, may hold values from 0 to 1
- tile_place: int32 [512, 8], P(('grp', 'tm')), parts along dimension 0, may hold values from 0 to 1023
- time_cov: float32 [128, 128], replicated, as said below
- lat_cov: float32 [128, 128], replicated
- lon_cov: float32 [128, 128], replicated
Outputs:
- solution: float32 [64, 4, 128], P(('grp', 'tm')), parts along dimension 0
- flux_update: float32 [256, 128, 4, 128], P(('grp', 'tm')), parts along dimension 0
There are 2 independent parts, one for each index of `grp`. A program takes and returns all parts, laid end to end along the dimension named above; an argument that names none is the same for every part. Nothing has to cross between parts.
Inputs may be any that keep to these rules, and one draw needn't show every extreme that they name: time_cov, lat_cov and lon_cov are symmetric positive definite with positive entries.
All inputs are finite; a program needn't handle non-finite values.
Results may differ from a plain program's by a relative error of at most 0.0074.
Values may be sent and summed in bfloat16 or wider, within the bound.
No kernel may reach another device: no remote copies, remote signals or barrier semaphores. Data moves between devices by JAX's collectives and lax.ppermute only.
A program may use at most 64 MiB of HBM per device.

v0:
```python
import jax
import jax.numpy as jnp
from jax import lax
from jax.sharding import PartitionSpec as P

LAT = 128
LON = 128
BLOCK_OBS = 128
SAMPLES = 4
ITERS = 2


precise = lax.Precision.HIGHEST


def solve_spd(matrix, target):
    factor = jnp.linalg.cholesky(matrix)
    halfway = lax.linalg.triangular_solve(factor, target, left_side=True, lower=True)
    return lax.linalg.triangular_solve(
        factor, halfway, left_side=True, lower=True, transpose_a=True
    )


def combine(vectors, weights):
    return jnp.einsum("nks,kj->njs", vectors, weights, precision=precise)


def local(right_sides, obs_var, footprint, tile_block, tile_place, time_cov, lat_cov, lon_cov):
    devices = lax.axis_size("tm")
    owned_blocks = right_sides.shape[0]
    steps_here = time_cov.shape[0] // devices
    rows_here = steps_here * LAT
    block_range = jnp.arange(owned_blocks, dtype=jnp.int32)
    owner_base = (jnp.arange(devices, dtype=jnp.int32) * owned_blocks)[:, None]
    row_range = jnp.arange(rows_here, dtype=jnp.int32)
    placer = (row_range[:, None] == tile_place.reshape(-1)[None, :]).astype(jnp.float32)
    requests = owner_base + tile_block

    def spread(blocks_bf):
        gathered = lax.all_gather(blocks_bf, "tm", axis=0, tiled=True)
        chosen = jnp.take(gathered, requests, axis=0)
        contrib = jnp.einsum(
            "ocks,ocsl->ockl", chosen, footprint, preferred_element_type=jnp.float32
        )
        flux_field = jnp.einsum(
            "rt,tkl->rkl", placer, contrib.reshape(-1, SAMPLES, LON), precision=precise
        )
        return flux_field.reshape(steps_here, LAT, SAMPLES, LON)

    def over_time(cell_slab):
        mixed_cells = jnp.einsum("st,tbkl->sbkl", time_cov, cell_slab, precision=precise)
        return lax.all_to_all(mixed_cells, "tm", split_axis=0, concat_axis=1, tiled=True)

    def apply_prior(flux_field):
        flux_field = jnp.einsum("ab,tbkl->takl", lat_cov, flux_field, precision=precise)
        flux_field = jnp.einsum("tbkl,lm->tbkm", flux_field, lon_cov, precision=precise)
        return over_time(lax.all_to_all(flux_field, "tm", split_axis=1, concat_axis=0, tiled=True))

    def residual_gram(residual):
        local_gram = jnp.einsum("nks,njs->kj", residual, residual, precision=precise)
        return lax.psum(local_gram, "tm")

    solution = jnp.zeros_like(right_sides)
    residual = right_sides
    direction = right_sides
    norm_now = residual_gram(residual)
    for step in range(ITERS):
        operate_flux_field = apply_prior(spread(direction.astype(jnp.bfloat16)))
        flat_rows = operate_flux_field.astype(jnp.bfloat16).reshape(rows_here, SAMPLES, LON)
        picked = jnp.take(flat_rows, tile_place, axis=0)
        partial_value = jnp.einsum(
            "ockl,ocsl->ocks", picked, footprint, preferred_element_type=jnp.float32
        )
        selector = (tile_block[:, :, None] == block_range).astype(jnp.float32)
        summed = jnp.einsum("ocb,ocks->obks", selector, partial_value, precision=precise)
        image = (
            lax.psum_scatter(
                summed.reshape(lax.axis_size("tm") * owned_blocks, SAMPLES, BLOCK_OBS),
                "tm",
                scatter_dimension=0,
                tiled=True,
            )
            + obs_var[:, None, :] * direction
        )
        local_curve = jnp.einsum("nks,njs->kj", direction, image, precision=precise)
        curvature = lax.psum(local_curve, "tm")
        step_size = solve_spd(curvature, norm_now)
        solution = solution + combine(direction, step_size)
        residual = residual - combine(image, step_size)
        norm_next = residual_gram(residual)
        mix_ratio = solve_spd(norm_now, norm_next)
        direction = residual + combine(direction, mix_ratio)
        norm_now = norm_next
    flux_update = apply_prior(spread(solution.astype(jnp.bfloat16)))
    return (solution, flux_update)


def solution(mesh):
    in_specs = (
        P(("grp", "tm"), None, None),
        P(("grp", "tm"), None),
        P(("grp", "tm"), None, None, None),
        P(("grp", "tm"), None),
        P(("grp", "tm"), None),
        P(),
        P(),
        P(),
    )
    out_specs = (P(("grp", "tm"), None, None), P(("grp", "tm"), None, None, None))
    return jax.shard_map(local, mesh=mesh, in_specs=in_specs, out_specs=out_specs, check_vma=False)
```

profile of v0, /device:TPU:0, one launch (start us, length us, event | category | flops | bytes accessed | tf_op | source)
XLA Modules:
  0.0 690.0 jit_solution(16104746419268049589)
XLA Ops:
  7.2 0.7 compare_and_fusion.1
  8.1 0.7 convert_element_type.38
  8.8 23.2 %all_gather.9 = bf16[32,4,128]{2,1,0:T(4,128)(2,1)S(1)} all-gather(bf16[2,4,128]{2,1,0:T(4,128)(2,1)S(1)} %convert_element_type.38), channel_id=1, replica_groups=mesh['grp'=2,'tm'=16] {'tm'}, dimensions={0}, use_global_device_ids=true | all-gather | bytes 34816 | tf_op jit(solution)/shard_map/all_gather | solution.py:40
  32.0 0.8 copy.195
  32.8 0.8 gather_fusion
  33.6 3.4 fusion.57
  37.0 1.2 fusion.28
  38.3 1.9 fusion.74
  40.2 3.5 fusion.4
  43.7 1.4 copy.201
  45.1 50.1 %all_to_all.90 = f32[8,128,4,128]{3,2,0,1:T(4,128)S(1)} all-to-all(f32[8,128,4,128]{3,2,0,1:T(4,128)S(1)} %copy.201), channel_id=1, replica_groups=mesh['grp'=2,'tm'=16] {'tm'}, dimensions={1} | all-to-all | bytes 4194304 | tf_op jit(solution)/shard_map/all_to_all | solution.py:57
  95.2 1.2 copy.321
  97.3 4.3 fusion.12
  101.5 1.7 copy.205
  103.2 4.9 all-to-all-start.1
  108.5 22.5 %all-to-all-done.1 = bf16[128,8,4,128]{3,2,1,0:T(4,128)(2,1)S(1)} async-done(((bf16[128,8,4,128]{3,2,1,0:T(4,128)(2,1)}), bf16[128,8,4,128]{3,2,1,0:T(4,128)(2,1)S(1)}, u32[]{:S(2)}, u32[]{:S(2)}) %all-to-all-start.1) | async-done | bytes 1048608 | tf_op jit(solution)/shard_map/all_to_all | solution.py:52
  131.5 0.8 copy.209
  132.4 0.7 gather_fusion.1
  133.2 4.5 fusion.55
  137.9 0.7 copy.212
  140.1 85.4 %all-reduce.6.cloned.1.call-done = f32[32,4,128]{2,1,0:T(4,128)} async-done(((f32[32,4,128]{2,1,0:T(4,128)}), f32[32,4,128]{2,1,0:T(4,128)}) %all-reduce.6.cloned.1.call-update) | async-done | bytes 65552
  225.5 0.8 convolution_bitcast_fusion.8
  226.3 31.7 %all-reduce.2 = (f32[4,4]{0,1:T(4,128)S(1)}, f32[4,4]{0,1:T(4,128)S(1)}) all-reduce(f32[4,4]{0,1:T(4,128)S(1)} %convolution_bitcast_fusion.7, f32[4,4]{0,1:T(4,128)S(1)} %convolution_bitcast_fusion.8), channel_id=1, replica_groups=mesh['grp'=2,'tm'=16] {'tm'}, use_global_device_ids=true, to_apply=%region_4.0 | all-reduce | flops 32 | bytes 256 | tf_op jit(solution)/shard_map/psum | solution.py:61
  258.6 0.6 compare_reduce_fusion.2
  259.3 0.6 fusion.86
  260.7 0.8 fusion.23
  261.6 29.5 %psum.30 = f32[4,4]{1,0:T(4,128)S(1)} all-reduce(f32[4,4]{1,0:T(4,128)S(1)} %convolution_bitcast_fusion.5), channel_id=1, replica_groups=mesh['grp'=2,'tm'=16] {'tm'}, use_global_device_ids=true, to_apply=%region_5.11 | all-reduce | flops 16 | bytes 128 | tf_op jit(solution)/shard_map/psum | solution.py:61
  291.5 0.6 compare_reduce_fusion.1
  292.2 0.6 fusion.87
  293.7 17.6 %all_gather.10 = bf16[32,4,128]{2,1,0:T(4,128)(2,1)S(1)} all-gather(bf16[2,4,128]{2,1,0:T(4,128)(2,1)S(1)} %get-tuple-element.17), channel_id=1, replica_groups=mesh['grp'=2,'tm'=16] {'tm'}, dimensions={0}, use_global_device_ids=true | all-gather | bytes 34816 | tf_op jit(solution)/shard_map/all_gather | solution.py:40
  311.3 0.7 gather_fusion.2
  312.0 3.4 fusion.53
  315.5 1.2 fusion.26
  316.7 1.9 fusion.72
  318.6 3.5 fusion.2
  322.1 1.4 copy.229
  323.5 50.7 %all_to_all.91 = f32[8,128,4,128]{3,2,0,1:T(4,128)S(1)} all-to-all(f32[8,128,4,128]{3,2,0,1:T(4,128)S(1)} %copy.229), channel_id=1, replica_groups=mesh['grp'=2,'tm'=16] {'tm'}, dimensions={1} | all-to-all | bytes 4194304 | tf_op jit(solution)/shard_map/all_to_all | solution.py:57
  374.1 1.2 copy.320
  375.6 4.3 fusion.15
  379.9 1.0 copy.233
  380.9 29.7 %all_to_all.92 = bf16[128,8,4,128]{3,2,1,0:T(4,128)(2,1)S(1)} all-to-all(bf16[128,8,4,128]{3,2,1,0:T(4,128)(2,1)S(1)} %copy.233), channel_id=1, replica_groups=mesh['grp'=2,'tm'=16] {'tm'}, dimensions={0} | all-to-all | bytes 2097152 | tf_op jit(solution)/shard_map/all_to_all | solution.py:52
  411.1 0.8 copy.237
  411.9 0.7 gather_fusion.3
  412.7 4.5 fusion.51
  417.5 0.7 copy.240
  418.1 84.9 %all-reduce.8.cloned.1.call-done = f32[32,4,128]{2,1,0:T(4,128)} async-done(((f32[32,4,128]{2,1,0:T(4,128)}), f32[32,4,128]{2,1,0:T(4,128)}) %all-reduce.8.cloned.1.call-update) | async-done | bytes 65552
  503.1 0.8 convolution_bitcast_fusion.3
  504.0 31.8 %psum.31 = f32[4,4]{0,1:T(4,128)S(1)} all-reduce(f32[4,4]{0,1:T(4,128)S(1)} %convolution_bitcast_fusion.3), channel_id=1, replica_groups=mesh['grp'=2,'tm'=16] {'tm'}, use_global_device_ids=true, to_apply=%region_7.13 | all-reduce | flops 16 | bytes 128 | tf_op jit(solution)/shard_map/psum | solution.py:86
  536.3 0.6 compare_reduce_fusion
  536.9 0.6 fusion.88
  538.3 0.8 fusion.113
  539.1 17.4 %all_gather.11 = bf16[32,4,128]{2,1,0:T(4,128)(2,1)S(1)} all-gather(bf16[2,4,128]{2,1,0:T(4,128)(2,1)S(1)} %get-tuple-element.19), channel_id=1, replica_groups=mesh['grp'=2,'tm'=16] {'tm'}, dimensions={0}, use_global_device_ids=true | all-gather | bytes 34816 | tf_op jit(solution)/shard_map/all_gather | solution.py:40
  556.5 0.7 gather_fusion.4
  557.2 3.4 fusion.49
  560.6 1.2 fusion.24
  561.9 1.9 fusion.70
  563.8 3.5 fusion
  567.3 1.4 copy.251
  568.7 50.7 %all_to_all.93 = f32[8,128,4,128]{3,2,0,1:T(4,128)S(1)} all-to-all(f32[8,128,4,128]{3,2,0,1:T(4,128)S(1)} %copy.251), channel_id=1, replica_groups=mesh['grp'=2,'tm'=16] {'tm'}, dimensions={1} | all-to-all | bytes 4194304 | tf_op jit(solution)/shard_map/all_to_all | solution.py:57
  619.4 1.2 copy.319
  620.9 4.3 fusion.18
  625.2 2.0 copy.255
  627.2 52.4 %all_to_all.94 = f32[128,8,4,128]{3,2,1,0:T(4,128)S(1)} all-to-all(f32[128,8,4,128]{3,2,1,0:T(4,128)} %copy.255), channel_id=1, replica_groups=mesh['grp'=2,'tm'=16] {'tm'}, dimensions={0} | all-to-all | bytes 4194304 | tf_op jit(solution)/shard_map/all_to_all | solution.py:52
  680.0 2.7 copy.258
  (70 shorter events, 8.9 us)
Async XLA Ops:
  7.2 31.1 %copy-start = (f32[128,128]{1,0:T(8,128)S(1)}, f32[128,128]{1,0:T(8,128)}, u32[]{:S(2)}) copy-start(f32[128,128]{1,0:T(8,128)} %param.23) | copy-start | bytes 196612
  38.3 1.9 copy-start.1
  96.4 0.8 copy-start.2
  101.5 6.7 copy-start.5
  101.5 6.7 copy-start.4
  103.2 27.9 %all-to-all-start.1 = ((bf16[128,8,4,128]{3,2,1,0:T(4,128)(2,1)}), bf16[128,8,4,128]{3,2,1,0:T(4,128)(2,1)S(1)}, u32[]{:S(2)}, u32[]{:S(2)}) async-start(bf16[128,8,4,128]{3,2,1,0:T(4,128)(2,1)} %copy.205), calls=%async_computation.1 | async-start | bytes 2097152 | tf_op jit(solution)/shard_map/all_to_all | solution.py:52
  108.1 117.3 %all-reduce.6.cloned.1.call-start = ((), (), s32[]{:S(2)}) async-start(), calls=%async_computation.6 | async-start | bytes 131072
  133.1 5.6 copy-start.3
  133.1 5.7 copy-start.7
  133.1 92.3 %copy-start.6 = (f32[2,128]{1,0:T(2,128)S(1)}, f32[2,128]{1,0:T(2,128)}, u32[]{:S(2)}) copy-start(f32[2,128]{1,0:T(2,128)} %param.18) | copy-start | bytes 3076
  138.6 364.5 %all-reduce.8.cloned.1.call-start = ((), (), s32[]{:S(2)}) async-start(), calls=%async_computation.7 | async-start | bytes 131072
Sparse Core Ops, SparseCore 0:
  138.7 86.6 all-reduce.5
  418.3 84.7 all-reduce.7
where the time goes:
time: 698 us; the launch traced here: 690 us
  blocking collectives  385 us (55%)
  waiting for transfers between devices  193 us (28%)
  matrix products  57.4 us (8%)
  local copies, waits for them, and re-layouts  26.8 us (4%)
  between operations  15.6 us (2%)
  other arithmetic  7.5 us (1%)
    unnamed x4, waiting for transfers between devices  170 us
    all_to_all x3, blocking collectives, apply_prior(): lax.all_to_all(flux_field, 'tm', split_axis=1, concat_axis=0, tiled=True)  152 us
    all_to_all x2, blocking collectives, over_time(): lax.all_to_all(mixed_cells, 'tm', split_axis=0, concat_axis=1, tiled=True)  82.2 us
    psum x2, blocking collectives, residual_gram(): return lax.psum(local_gram, 'tm')  61.2 us
    all_gather x3, blocking collectives, spread(): gathered = lax.all_gather(blocks_bf, 'tm', axis=0, tiled=True)  58.2 us
    psum x1, blocking collectives, local(): curvature = lax.psum(local_curve, 'tm')  31.8 us
    all_to_all x1, waiting for transfers between devices, over_time(): lax.all_to_all(mixed_cells, 'tm', split_axis=0, concat_axis=1, tiled=True)  22.5 us
  transfers between devices with their start and end apart: 3, of which 3 were waited for; matrix products, arithmetic and copies ran while one was open for 0% of the time, Pallas kernels for 0%

commit v1 on v0

v1 whole, which is shorter than its diff:
```python
import jax
import jax.numpy as jnp
from jax import lax
from jax.sharding import PartitionSpec as P

LAT = 128
LON = 128
BLOCK_OBS = 128
SAMPLES = 4
ITERS = 2


precise = lax.Precision.HIGHEST
high = lax.Precision.HIGH


def solve_spd(matrix, target):
    factor = jnp.linalg.cholesky(matrix)
    halfway = lax.linalg.triangular_solve(factor, target, left_side=True, lower=True)
    return lax.linalg.triangular_solve(
        factor, halfway, left_side=True, lower=True, transpose_a=True
    )


def combine(vectors, weights):
    return jnp.einsum("nks,kj->njs", vectors, weights, precision=precise)


def gram(left, right):
    return jnp.einsum("nks,njs->kj", left, right, precision=precise)


def to_all(array):
    devices = lax.axis_size("tm")
    copies = jnp.broadcast_to(array[None], (devices,) + array.shape)
    return lax.all_to_all(copies, "tm", split_axis=0, concat_axis=0, tiled=True)


def local(right_sides, obs_var, footprint, tile_block, tile_place, time_cov, lat_cov, lon_cov):
    devices = lax.axis_size("tm")
    me = lax.axis_index("tm")
    owned = right_sides.shape[0]
    blocks = devices * owned
    steps_here = time_cov.shape[0] // devices
    slots = tile_block.shape[1]
    tiles = devices * slots
    rows_here = steps_here * LAT
    owner_base = (jnp.arange(devices, dtype=jnp.int32) * owned)[:, None]
    requests = owner_base + tile_block

    packed = jnp.concatenate(
        [
            right_sides.reshape(-1, 128),
            obs_var.reshape(-1, 128),
            tile_place.astype(jnp.float32).reshape(-1, 128),
        ]
    )
    everyone = to_all(packed)
    at = owned * SAMPLES
    rhs = everyone[:, :at].reshape(blocks, SAMPLES, BLOCK_OBS)
    variance = everyone[:, at : at + owned].reshape(blocks, BLOCK_OBS)
    places = everyone[:, at + owned :].reshape(devices, tiles).astype(jnp.int32)
    times = (places // LAT + steps_here * jnp.arange(devices, dtype=jnp.int32)[:, None]).reshape(-1)
    rows = (places % LAT).reshape(-1)
    time_hot = (jnp.arange(time_cov.shape[0])[:, None] == times[None, :]).astype(jnp.float32)
    row_hot = (jnp.arange(LAT)[:, None] == rows[None, :]).astype(jnp.float32)
    my_times = lax.dynamic_slice_in_dim(time_cov, me * steps_here, steps_here, 0)
    time_part = jnp.dot(my_times, time_hot, precision=precise)
    row_part = jnp.dot(lat_cov, row_hot, precision=precise)
    dense = (time_part[:, None, :] * row_part[None, :, :]).astype(jnp.bfloat16)
    dense = dense.reshape(rows_here, devices * tiles)
    mine = jnp.take(dense, tile_place.reshape(-1), axis=0)

    def spread(vectors):
        chosen = jnp.take(vectors.astype(jnp.bfloat16), requests, axis=0)
        contrib = jnp.einsum(
            "ocks,ocsl->ockl", chosen, footprint, preferred_element_type=jnp.float32
        )
        contrib = contrib.astype(jnp.bfloat16).reshape(tiles, SAMPLES * LON)
        return lax.all_gather(contrib, "tm", axis=0, tiled=True)

    def collect(gathered):
        field = jnp.dot(mine, gathered, preferred_element_type=jnp.float32)
        field = jnp.dot(field.reshape(-1, LON), lon_cov, precision=precise)
        picked = field.astype(jnp.bfloat16).reshape(devices, slots, SAMPLES, LON)
        partial = jnp.einsum(
            "ockl,ocsl->ocks", picked, footprint, preferred_element_type=jnp.float32
        )
        block_range = jnp.arange(owned, dtype=jnp.int32)
        selector = (tile_block[:, :, None] == block_range).astype(jnp.float32)
        summed = jnp.einsum("ocb,ocks->obks", selector, partial, precision=precise)
        terms = lax.all_to_all(
            summed.reshape(devices, owned * SAMPLES, BLOCK_OBS), "tm", 0, 0, tiled=True
        )
        return to_all(terms.sum(0)).reshape(blocks, SAMPLES, BLOCK_OBS)

    solution = jnp.zeros_like(rhs)
    residual = rhs
    direction = rhs
    norm_now = gram(rhs, rhs)
    gathers, sizes = [], []
    for step in range(ITERS):
        gathered = spread(direction)
        image = collect(gathered) + variance[:, None, :] * direction
        step_size = solve_spd(gram(direction, image), norm_now)
        gathers.append(gathered)
        sizes.append(step_size)
        solution = solution + combine(direction, step_size)
        if step + 1 == ITERS:
            break
        residual = residual - combine(image, step_size)
        norm_next = gram(residual, residual)
        mix_ratio = solve_spd(norm_now, norm_next)
        direction = residual + combine(direction, mix_ratio)
        norm_now = norm_next

    def mix(gathered, size):
        whole = gathered.astype(jnp.float32).reshape(-1, SAMPLES, LON)
        return jnp.einsum("tkl,kj->tjl", whole, size, precision=precise)

    def apply_dense(gathered):
        return jnp.dot(dense, gathered, preferred_element_type=jnp.float32)

    if rows_here < devices * tiles // 4:
        flux = sum(mix(apply_dense(g), size) for g, size in zip(gathers, sizes))
    else:
        total = sum(mix(g, size) for g, size in zip(gathers, sizes))
        flux = apply_dense(total.astype(jnp.bfloat16).reshape(-1, SAMPLES * LON))
    flux = jnp.dot(flux.reshape(-1, LON), lon_cov, precision=precise)
    mine_now = lax.dynamic_slice_in_dim(solution, me * owned, owned, 0)
    return (mine_now, flux.reshape(steps_here, LAT, SAMPLES, LON))


def solution(mesh):
    in_specs = (
        P(("grp", "tm"), None, None),
        P(("grp", "tm"), None),
        P(("grp", "tm"), None, None, None),
        P(("grp", "tm"), None),
        P(("grp", "tm"), None),
        P(),
        P(),
        P(),
    )
    out_specs = (P(("grp", "tm"), None, None), P(("grp", "tm"), None, None, None))
    return jax.shard_map(local, mesh=mesh, in_specs=in_specs, out_specs=out_specs, check_vma=False)
```

time: 698 us -> 205 us (0.29); the launches traced: 690 us -> 204 us
  blocking collectives: 385 us -> 0 us
  waiting for transfers between devices: 193 us -> 90.1 us
  starting transfers between devices: 4.99 us -> 22.2 us
  matrix products: 57.4 us -> 43.4 us
    all_to_all x5 -> x0, blocking collectives: 234 us -> none  [the longest x3 152 us: apply_prior(): lax.all_to_all(flux_field, 'tm', split_axis=1, concat_axis=0, tiled=True)]
    unnamed x4 -> x2, waiting for transfers between devices: 170 us -> 0.03 us
    psum x3 -> x0, blocking collectives: 93 us -> none  [the longest x2 61.2 us: residual_gram(): return lax.psum(local_gram, 'tm')]
    all_gather x0 -> x2, waiting for transfers between devices: none -> 65.3 us  [spread(): return lax.all_gather(contrib, 'tm', axis=0, tiled=True)]
    all_gather x3 -> x0, blocking collectives: 58.2 us -> none  [spread(): gathered = lax.all_gather(blocks_bf, 'tm', axis=0, tiled=True)]
    all_to_all x1 -> x5, starting transfers between devices: 4.9 us -> 21.9 us  [the longest x3 14.9 us: to_all(): return lax.all_to_all(copies, 'tm', split_axis=0, concat_axis=0, tiled=True)]
    dot_general x20 -> x18, matrix products: 44.1 us -> 34 us  [the longest x2 10.6 us: mix(): return jnp.einsum('tkl,kj->tjl', whole, size, precision=precise)]
    all_to_all x1 -> x5, waiting for transfers between devices: 22.5 us -> 24.8 us  [the longest x3 16.6 us: to_all(): return lax.all_to_all(copies, 'tm', split_axis=0, concat_axis=0, tiled=True)]
  transfers between devices with their start and end apart: 3 -> 7, of which waited for: 3 -> 7; matrix products, arithmetic and copies ran while one was open for 0% -> 11% of each run, Pallas kernels for 0% -> 0%
where the time goes in v1:
time: 205 us; the launch traced here: 204 us
  waiting for transfers between devices  90.1 us (44%)
  matrix products  43.4 us (21%)
  starting transfers between devices  22.2 us (11%)
  local copies, waits for them, and re-layouts  21.7 us (11%)
  between operations  14.5 us (7%)
  other arithmetic  12.2 us (6%)
    all_gather x2, waiting for transfers between devices, spread(): return lax.all_gather(contrib, 'tm', axis=0, tiled=True)  65.3 us
    all_to_all x3, waiting for transfers between devices, to_all(): return lax.all_to_all(copies, 'tm', split_axis=0, concat_axis=0, tiled=True)  16.6 us
    all_to_all x3, starting transfers between devices, to_all(): return lax.all_to_all(copies, 'tm', split_axis=0, concat_axis=0, tiled=True)  14.9 us
    dot_general x2, matrix products, mix(): return jnp.einsum('tkl,kj->tjl', whole, size, precision=precise)  10.6 us
    dot_general x2, matrix products, collect(): jnp.einsum('ockl,ocsl->ocks', picked, footprint, preferred_element_type=j...  9.01 us
    all_to_all x2, waiting for transfers between devices, collect(): lax.all_to_all(summed.reshape(devices, owned * SAMPLES, BLOCK_OBS), 'tm',...  8.18 us
    dot_general x2, matrix products, spread(): jnp.einsum('ocks,ocsl->ockl', chosen, footprint, preferred_element_type=j...  7.04 us
    all_to_all x2, starting transfers between devices, collect(): lax.all_to_all(summed.reshape(devices, owned * SAMPLES, BLOCK_OBS), 'tm',...  7 us
  transfers between devices with their start and end apart: 7, of which 7 were waited for; matrix products, arithmetic and copies ran while one was open for 11% of the time, Pallas kernels for 0%

profile of v1, /device:TPU:0, one launch (start us, length us, event | category | flops | bytes accessed | tf_op | source)
XLA Modules:
  0.0 204.0 jit_solution(7115879556098147395)
XLA Ops:
  7.2 0.7 convert_element_type.56
  8.1 0.7 pad_maximum_fusion
  8.8 0.7 broadcast_in_dim.25
  9.4 7.4 %all-to-all-start = ((f32[16,11,128]{2,1,0:T(8,128)}), f32[16,11,128]{2,1,0:T(8,128)S(1)}, u32[]{:S(2)}, u32[]{:S(2)}) async-start(f32[16,11,128]{2,1,0:T(8,128)} %broadcast_in_dim.25), calls=%async_computation | async-start | bytes 262144 | tf_op jit(solution)/shard_map/all_to_all | solution.py:36
  16.9 0.7 compare_and_fusion
  17.9 6.9 %all-to-all-done = f32[16,11,128]{2,1,0:T(8,128)S(1)} async-done(((f32[16,11,128]{2,1,0:T(8,128)}), f32[16,11,128]{2,1,0:T(8,128)S(1)}, u32[]{:S(2)}, u32[]{:S(2)}) %all-to-all-start) | async-done | bytes 90144 | tf_op jit(solution)/shard_map/all_to_all | solution.py:36
  24.8 0.7 gather_fusion.1
  25.6 3.5 %fusion.2 = bf16[16,8,4,128]{3,2,1,0:T(4,128)(2,1)S(1)} fusion(bf16[16,8,128,128]{3,2,1,0:T(8,128)(2,1)} %param.17, bf16[16,8,4,128]{3,2,1,0:T(4,128)(2,1)S(1)} %bitcast.200, pred[16,8]{1,0:T(8,128)(4,1)S(1)} %copy.65), kind=kOutput, calls=%fused_computation.13 | convolution fusion | flops 16908288 | bytes 4456576 | tf_op jit(solution)/shard_map/ocks,ocsl->ockl/dot_general | solution.py:76
  29.0 0.7 copy.110
  30.2 0.7 convolution_bitcast_fusion
  30.9 0.3 copy.63
  31.3 0.4 convolution_bitcast_fusion.8
  31.7 0.4 cholesky.70
  32.2 1.1 fusion.7
  33.3 3.0 %multiply_convert_fusion = bf16[8,128,2048]{2,1,0:T(8,128)(2,1)} fusion(f32[128,2048]{1,0:T(8,128)S(1)} %copy.63, f32[8,2048]{1,0:T(8,128)S(1)} %fusion.7), kind=kLoop, calls=%fused_computation.3 | loop fusion | flops 4194304 | bytes 5308416 | tf_op jit(solution)/shard_map/convert_element_type | solution.py:70
  36.3 4.2 %gather_fusion = bf16[128,2048]{1,0:T(8,128)(2,1)S(1)} fusion(bf16[1024,2048]{1,0:T(8,128)(2,1)} %bitcast.176, s32[1024]{0:T(1024)S(1)} %pad_clamp_fusion.1), kind=kCustom, calls=%fused_computation.2 | custom fusion | bytes 1049088 | tf_op jit(solution)/shard_map/jit(_take)/gather | solution.py:72
  40.5 28.5 %all-gather.3.cloned.1.call-done = bf16[2048,512]{1,0:T(8,128)(2,1)} async-done(((bf16[128,512]{1,0:T(8,128)(2,1)}), bf16[2048,512]{1,0:T(8,128)(2,1)}) %all-gather.3.cloned.1.call-update) | async-done | bytes 2097168 | tf_op jit(solution)/shard_map/all_gather | solution.py:80
  69.0 2.1 %fusion.16 = f32[128,512]{1,0:T(8,128)S(1)} fusion(bf16[2048,512]{1,0:T(8,128)(2,1)} %all-gather.3.cloned.1.call-done, bf16[128,2048]{1,0:T(8,128)(2,1)S(1)} %gather_fusion, pred[128]{0:T(512)(128)(4,1)S(1)} %compare_and_fusion.1), kind=kOutput, calls=%fused_computation.38 | convolution fusion | flops 268697600 | bytes 2883712 | tf_op jit(solution)/shard_map/dot_general | solution.py:83
  71.1 0.4 convolution_convert_fusion.3
  71.5 4.4 %fusion.63 = f32[16,8,4,128]{3,2,1,0:T(4,128)S(1)} fusion(bf16[16,8,4,128]{3,2,1,0:T(4,128)(2,1)S(1)} %bitcast.187, bf16[16,8,128,128]{3,2,1,0:T(8,128)(2,1)} %param.17), kind=kOutput, calls=%fused_computation.121 | convolution fusion | flops 16777216 | bytes 4587520 | tf_op jit(solution)/shard_map/ockl,ocsl->ocks/dot_general | solution.py:86
  76.2 0.7 copy.69
  76.9 3.5 %all-to-all-start.1 = ((f32[16,8,128]{2,1,0:T(8,128)}), f32[16,8,128]{2,1,0:T(8,128)S(1)}, u32[]{:S(2)}, u32[]{:S(2)}) async-start(f32[16,8,128]{2,1,0:T(8,128)} %copy.69), calls=%async_computation.1 | async-start | bytes 131072 | tf_op jit(solution)/shard_map/all_to_all | solution.py:92
  80.4 0.6 compare_reduce_fusion.1
  81.0 6.2 %all-to-all-done.1 = f32[16,8,128]{2,1,0:T(8,128)S(1)} async-done(((f32[16,8,128]{2,1,0:T(8,128)}), f32[16,8,128]{2,1,0:T(8,128)S(1)}, u32[]{:S(2)}, u32[]{:S(2)}) %all-to-all-start.1) | async-done | bytes 65568 | tf_op jit(solution)/shard_map/all_to_all | solution.py:92
  87.3 0.6 broadcast_in_dim.28
  87.9 3.5 %all-to-all-start.2 = ((f32[16,8,128]{2,1,0:T(8,128)}), f32[16,8,128]{2,1,0:T(8,128)S(1)}, u32[]{:S(2)}, u32[]{:S(2)}) async-start(f32[16,8,128]{2,1,0:T(8,128)} %broadcast_in_dim.28), calls=%async_computation.2 | async-start | bytes 131072 | tf_op jit(solution)/shard_map/all_to_all | solution.py:36
  91.7 0.7 fusion.42
  92.3 0.3 custom-call.15
  92.7 5.6 %all-to-all-done.2 = f32[16,8,128]{2,1,0:T(8,128)S(1)} async-done(((f32[16,8,128]{2,1,0:T(8,128)}), f32[16,8,128]{2,1,0:T(8,128)S(1)}, u32[]{:S(2)}, u32[]{:S(2)}) %all-to-all-start.2) | async-done | bytes 65568 | tf_op jit(solution)/shard_map/all_to_all | solution.py:36
  98.3 0.4 convolution_bitcast_fusion.9
  98.8 0.4 cholesky.59
  99.2 0.6 compare_reduce_fusion.2
  99.9 0.6 fusion.41
  100.5 0.3 custom-call.13
  101.5 0.4 convolution_bitcast_fusion.6
  102.3 0.3 fusion.62
  102.6 0.7 gather_fusion.2
  103.4 3.6 %fusion.3 = bf16[16,8,4,128]{3,2,1,0:T(4,128)(2,1)S(1)} fusion(bf16[16,8,128,128]{3,2,1,0:T(8,128)(2,1)} %param.17, bf16[16,8,4,128]{3,2,1,0:T(4,128)(2,1)S(1)} %bitcast.199, pred[16,8]{1,0:T(8,128)(4,1)S(1)} %copy.65), kind=kOutput, calls=%fused_computation.14 | convolution fusion | flops 16908288 | bytes 4456576 | tf_op jit(solution)/shard_map/ocks,ocsl->ockl/dot_general | solution.py:76
  106.9 0.7 copy.109
  107.7 2.0 reshape.203
  109.7 36.8 %all-gather.5.cloned.1.call-done = bf16[2048,512]{1,0:T(8,128)(2,1)} async-done(((bf16[128,512]{1,0:T(8,128)(2,1)}), bf16[2048,512]{1,0:T(8,128)(2,1)}) %all-gather.5.cloned.1.call-update) | async-done | bytes 2097168 | tf_op jit(solution)/shard_map/all_gather | solution.py:80
  146.5 2.1 %fusion.15 = f32[128,512]{1,0:T(8,128)S(1)} fusion(bf16[2048,512]{1,0:T(8,128)(2,1)} %all-gather.5.cloned.1.call-done, bf16[128,2048]{1,0:T(8,128)(2,1)S(1)} %gather_fusion, pred[128]{0:T(512)(128)(4,1)S(1)} %compare_and_fusion.1), kind=kOutput, calls=%fused_computation.37 | convolution fusion | flops 268697600 | bytes 2883712 | tf_op jit(solution)/shard_map/dot_general | solution.py:83
  148.6 0.4 convolution_convert_fusion.2
  148.9 4.6 %fusion.65 = f32[16,8,4,128]{3,2,1,0:T(4,128)S(1)} fusion(bf16[16,8,4,128]{3,2,1,0:T(4,128)(2,1)S(1)} %bitcast.188, bf16[16,8,128,128]{3,2,1,0:T(8,128)(2,1)} %param.17), kind=kOutput, calls=%fused_computation.123 | convolution fusion | flops 16777216 | bytes 4587520 | tf_op jit(solution)/shard_map/ockl,ocsl->ocks/dot_general | solution.py:86
  153.8 0.6 copy.83
  154.5 3.5 %all-to-all-start.3 = ((f32[16,8,128]{2,1,0:T(8,128)}), f32[16,8,128]{2,1,0:T(8,128)S(1)}, u32[]{:S(2)}, u32[]{:S(2)}) async-start(f32[16,8,128]{2,1,0:T(8,128)} %copy.83), calls=%async_computation.3 | async-start | bytes 131072 | tf_op jit(solution)/shard_map/all_to_all | solution.py:92
  158.0 4.9 %fusion.67 = f32[4,2048,128]{2,0,1:T(4,128)} fusion(f32[4,4,1]{0,1,2:T(4,128)S(1)} %convolution_bitcast_fusion.7, bf16[2048,4,128]{2,1,0:T(4,128)(2,1)S(1)} %copy-done.2), kind=kOutput, calls=%fused_computation.125 | convolution fusion | flops 50331648 | bytes 6291520 | tf_op jit(solution)/shard_map/tkl,kj->tjl/dot_general | solution.py:119
  162.9 2.0 all-to-all-done.3
  164.9 0.6 broadcast_in_dim.29
  165.5 4.0 %all-to-all-start.4 = ((f32[16,8,128]{2,1,0:T(8,128)}), f32[16,8,128]{2,1,0:T(8,128)S(1)}, u32[]{:S(2)}, u32[]{:S(2)}) async-start(f32[16,8,128]{2,1,0:T(8,128)} %broadcast_in_dim.29), calls=%async_computation.4 | async-start | bytes 131072 | tf_op jit(solution)/shard_map/all_to_all | solution.py:36
  169.8 2.6 %reshape.204 = bf16[2048,4,128]{2,1,0:T(4,128)(2,1)S(1)} reshape(bf16[2048,512]{1,0:T(8,128)(2,1)} %all-gather.5.cloned.1.call-done) | data formatting | bytes 4194304 | tf_op jit(solution)/shard_map/reshape | solution.py:118
  172.4 4.1 %all-to-all-done.4 = f32[16,8,128]{2,1,0:T(8,128)S(1)} async-done(((f32[16,8,128]{2,1,0:T(8,128)}), f32[16,8,128]{2,1,0:T(8,128)S(1)}, u32[]{:S(2)}, u32[]{:S(2)}) %all-to-all-start.4) | async-done | bytes 65568 | tf_op jit(solution)/shard_map/all_to_all | solution.py:36
  176.4 0.4 convolution_bitcast_fusion.4
  176.9 0.4 cholesky.81
  177.3 0.6 compare_reduce_fusion
  178.0 0.6 fusion.43
  178.6 0.3 custom-call.17
  179.7 5.7 %add_convert_fusion = bf16[4,2048,128]{2,0,1:T(4,128)(2,1)S(1)} fusion(f32[4,2048,128]{2,0,1:T(4,128)} %fusion.67, f32[4,4,1]{0,1,2:T(4,128)S(1)} %convolution_bitcast_fusion.3, bf16[2048,4,128]{2,1,0:T(4,128)(2,1)S(1)} %reshape.204), kind=kOutput, calls=%fused_computation.6 | convolution fusion | flops 52428800 | bytes 8388672 | tf_op jit(solution)/shard_map/tkl,kj->tjl/dot_general | solution.py:119
  185.3 0.4 copy.108
  185.7 2.4 %copy.90 = bf16[512,2048]{1,0:T(8,128)(2,1)} copy(bf16[512,2048]{0,1:T(8,128)(2,1)S(1)} %bitcast.178) | data formatting | bytes 4194304 | tf_op jit(solution)/shard_map/dot_general | solution.py:122
  188.1 3.9 %fusion = f32[8,128,4,128]{3,1,2,0:T(8,128)S(1)} fusion(bf16[4,128,2048,1]{2,1,0,3:T(8,128)(2,1)} %bitcast.185, f32[128,2048]{1,0:T(8,128)S(1)} %copy-done.4, f32[8,2048]{1,0:T(8,128)S(1)} %fusion.7), kind=kOutput, calls=%fused_computation.4 | convolution fusion | flops 2151677952 | bytes 5308416 | tf_op jit(solution)/shard_map/dot_general | solution.py:122
  192.0 1.8 fusion.21
  193.9 2.7 %copy.91 = f32[8,128,4,128]{3,2,1,0:T(4,128)} copy(f32[8,128,4,128]{3,1,2,0:T(8,128)S(1)} %fusion.21) | data formatting | bytes 4194304
  196.6 0.6 fusion.39
  (68 shorter events, 4.3 us)
Async XLA Ops:
  7.2 63.9 %copy-start = (f32[128,128]{1,0:T(8,128)S(1)}, f32[128,128]{1,0:T(8,128)}, u32[]{:S(2)}) copy-start(f32[128,128]{1,0:T(8,128)} %param.22) | copy-start | bytes 196612
  9.4 15.3 %all-to-all-start = ((f32[16,11,128]{2,1,0:T(8,128)}), f32[16,11,128]{2,1,0:T(8,128)S(1)}, u32[]{:S(2)}, u32[]{:S(2)}) async-start(f32[16,11,128]{2,1,0:T(8,128)} %broadcast_in_dim.25), calls=%async_computation | async-start | bytes 262144 | tf_op jit(solution)/shard_map/all_to_all | solution.py:36
  16.8 52.1 %all-gather.3.cloned.1.call-start = ((), (), s32[]{:S(2)}) async-start(), calls=%async_computation.5 | async-start | bytes 2228224 | tf_op jit(solution)/shard_map/all_gather | solution.py:80
  25.5 4.2 %copy-start.6 = (s32[16,8]{0,1:T(8,128)S(1)}, s32[16,8]{0,1:T(8,128)}, u32[]{:S(2)}) copy-start(s32[16,8]{0,1:T(8,128)} %param.19) | copy-start | bytes 1540
  25.6 4.5 %copy-start.7 = (s32[16,8]{0,1:T(8,128)S(1)}, s32[16,8]{0,1:T(8,128)}, u32[]{:S(2)}) copy-start(s32[16,8]{0,1:T(8,128)} %param.18) | copy-start | bytes 1540
  25.6 4.7 %copy-start.5 = (f32[128,128]{1,0:T(8,128)S(1)}, f32[128,128]{1,0:T(8,128)}, u32[]{:S(2)}) copy-start(f32[128,128]{1,0:T(8,128)} %param.21) | copy-start | bytes 196612
  31.3 5.1 %copy-start.3 = (f32[128,2048]{1,0:T(8,128)}, f32[128,2048]{1,0:T(8,128)S(1)}, u32[]{:S(2)}) copy-start(f32[128,2048]{1,0:T(8,128)S(1)} %copy.63) | copy-start | bytes 3145732
  76.9 10.4 %all-to-all-start.1 = ((f32[16,8,128]{2,1,0:T(8,128)}), f32[16,8,128]{2,1,0:T(8,128)S(1)}, u32[]{:S(2)}, u32[]{:S(2)}) async-start(f32[16,8,128]{2,1,0:T(8,128)} %copy.69), calls=%async_computation.1 | async-start | bytes 131072 | tf_op jit(solution)/shard_map/all_to_all | solution.py:92
  87.9 10.4 %all-to-all-start.2 = ((f32[16,8,128]{2,1,0:T(8,128)}), f32[16,8,128]{2,1,0:T(8,128)S(1)}, u32[]{:S(2)}, u32[]{:S(2)}) async-start(f32[16,8,128]{2,1,0:T(8,128)} %broadcast_in_dim.28), calls=%async_computation.2 | async-start | bytes 131072 | tf_op jit(solution)/shard_map/all_to_all | solution.py:36
  91.4 55.0 %all-gather.5.cloned.1.call-start = ((), (), s32[]{:S(2)}) async-start(), calls=%async_computation.6 | async-start | bytes 2228224 | tf_op jit(solution)/shard_map/all_gather | solution.py:80
  103.4 4.3 %copy-start.1 = (bf16[2048,512]{1,0:T(8,128)(2,1)S(1)}, bf16[2048,512]{1,0:T(8,128)(2,1)}, u32[]{:S(2)}) copy-start(bf16[2048,512]{1,0:T(8,128)(2,1)} %all-gather.3.cloned.1.call-done) | copy-start | bytes 6291460
  148.9 9.0 %copy-start.2 = (bf16[2048,4,128]{2,1,0:T(4,128)(2,1)S(1)}, bf16[2048,4,128]{2,1,0:T(4,128)(2,1)}, u32[]{:S(2)}) copy-start(bf16[2048,4,128]{2,1,0:T(4,128)(2,1)} %reshape.203) | copy-start | bytes 6291460
  154.5 10.4 %all-to-all-start.3 = ((f32[16,8,128]{2,1,0:T(8,128)}), f32[16,8,128]{2,1,0:T(8,128)S(1)}, u32[]{:S(2)}, u32[]{:S(2)}) async-start(f32[16,8,128]{2,1,0:T(8,128)} %copy.83), calls=%async_computation.3 | async-start | bytes 131072 | tf_op jit(solution)/shard_map/all_to_all | solution.py:92
  165.5 10.9 %all-to-all-start.4 = ((f32[16,8,128]{2,1,0:T(8,128)}), f32[16,8,128]{2,1,0:T(8,128)S(1)}, u32[]{:S(2)}, u32[]{:S(2)}) async-start(f32[16,8,128]{2,1,0:T(8,128)} %broadcast_in_dim.29), calls=%async_computation.4 | async-start | bytes 131072 | tf_op jit(solution)/shard_map/all_to_all | solution.py:36
  185.7 2.4 %copy-start.4 = (f32[128,2048]{1,0:T(8,128)S(1)}, f32[128,2048]{1,0:T(8,128)}, u32[]{:S(2)}) copy-start(f32[128,2048]{1,0:T(8,128)} %copy-done.3) | copy-start | bytes 3145732
Sparse Core Ops, SparseCore 0:
  29.9 39.0 all-gather.2
  107.8 38.6 all-gather.4

commit v2 on v1

--- a/solution.py
+++ b/solution.py
@@ -1,6 +1,10 @@
+import functools
+
 import jax
 import jax.numpy as jnp
 from jax import lax
+from jax.experimental import pallas as pl
+from jax.experimental.pallas import tpu as pltpu
 from jax.sharding import PartitionSpec as P
 
 LAT = 128
@@ -11,7 +15,6 @@
 
 
 precise = lax.Precision.HIGHEST
-high = lax.Precision.HIGH
 
 
 def solve_spd(matrix, target):
@@ -36,7 +39,9 @@
     return lax.all_to_all(copies, "tm", split_axis=0, concat_axis=0, tiled=True)
 
 
-def local(right_sides, obs_var, footprint, tile_block, tile_place, time_cov, lat_cov, lon_cov):
+def by_gather(
+    right_sides, obs_var, footprint, tile_block, tile_place, time_cov, lat_cov, lon_cov
+):
     devices = lax.axis_size("tm")
     me = lax.axis_index("tm")
     owned = right_sides.shape[0]
@@ -131,6 +136,476 @@
     return (mine_now, flux.reshape(steps_here, LAT, SAMPLES, LON))
 
 
+def rolled(x, shift):
+    return x if shift == 0 else pltpu.roll(x, 8 - 2 * shift, x.ndim - 2)
+
+
+def row_gram(left, right):
+    entry = [[None] * SAMPLES for _ in range(SAMPLES)]
+    for shift in range(SAMPLES):
+        product = jnp.sum(left * rolled(right, shift), axis=0)
+        total = jnp.broadcast_to(jnp.sum(product, axis=1, keepdims=True), product.shape)
+        for k in range(SAMPLES):
+            pair = total[2 * k : 2 * k + 1] + total[2 * k + 1 : 2 * k + 2]
+            entry[k][(k + shift) % SAMPLES] = pair
+    return entry
+
+
+def row_solve(matrix, target):
+    size = range(SAMPLES)
+    sym = [[0.5 * (matrix[i][j] + matrix[j][i]) for j in size] for i in size]
+    low = [[None] * SAMPLES for _ in size]
+    scaled = [[None] * SAMPLES for _ in size]
+    inverse = []
+    for j in size:
+        pivot = sym[j][j]
+        for p in range(j):
+            pivot = pivot - low[j][p] * scaled[j][p]
+        inverse.append(1.0 / pivot)
+        for i in range(j + 1, SAMPLES):
+            value = sym[i][j]
+            for p in range(j):
+                value = value - scaled[i][p] * low[j][p]
+            scaled[i][j] = value
+            low[i][j] = value * inverse[j]
+    out = [[None] * SAMPLES for _ in size]
+    for c in size:
+        part = []
+        for i in size:
+            value = target[i][c]
+            for p in range(i):
+                value = value - low[i][p] * part[p]
+            part.append(value)
+        for i in reversed(size):
+            value = part[i] * inverse[i]
+            for p in range(i + 1, SAMPLES):
+                value = value - low[p][i] * out[p][c]
+            out[i][c] = value
+    return out
+
+
+def row_weights(weights):
+    sample = lax.broadcasted_iota(jnp.int32, (8, 128), 0) // 2
+    result = []
+    for shift in range(SAMPLES):
+        rows = jnp.broadcast_to(weights[shift][0], (8, 128))
+        for j in range(1, SAMPLES):
+            rows = jnp.where(sample == j, weights[(j + shift) % SAMPLES][j], rows)
+        result.append(rows)
+    return result
+
+
+def row_combine(x, per_shift):
+    total = 0.0
+    for shift in range(SAMPLES):
+        total = total + rolled(x, shift) * per_shift[shift]
+    return total
+
+
+def spread_tiles(step, owners, vectors, footprint, products, split):
+    slots = footprint.shape[1]
+    for q in range(owners):
+        owner = step * owners + q
+        rows = vectors[owner]
+        lhs = rows.astype(jnp.bfloat16)
+        if split:
+            upper = lhs.astype(jnp.float32)
+            lhs = jnp.concatenate([upper, rows - upper], axis=0).astype(jnp.bfloat16)
+        for c in range(slots):
+            r = jnp.dot(lhs, footprint[q, c], preferred_element_type=jnp.float32)
+            products[owner * slots + c] = r[:8] + r[8:] if split else r
+
+
+def spread_end(products, second, lon, by_column, by_tile):
+    width = by_column.shape[1]
+    chunks = LON // width
+    for k in range(SAMPLES):
+        chosen = jnp.where(second, products[:, 2 * k + 1, :], products[:, 2 * k, :])
+        mixed = jnp.dot(
+            chosen, lon[...], precision=precise, preferred_element_type=jnp.float32
+        )
+        by_tile[:, k * LON : (k + 1) * LON] = mixed.astype(jnp.bfloat16)
+        turned = mixed.T.astype(jnp.bfloat16)
+        by_column[k * chunks : (k + 1) * chunks] = turned.reshape(chunks, width, LON)
+
+
+def first_body(owners, everyone, second, lon, footprint, by_column, by_tile, products):
+    step = pl.program_id(0)
+    vectors = everyone.at[:, 0:8, :]
+    spread_tiles(step, owners, vectors, footprint, products, False)
+
+    @pl.when(step == pl.num_programs(0) - 1)
+    def _():
+        spread_end(products, second[...] == 1, lon, by_column, by_tile)
+
+
+def update_body(
+    owners, everyone, image_in, second, lon, footprint,
+    by_column, by_tile, direction, sizes, norm, products,
+):
+    step = pl.program_id(0)
+
+    @pl.when(step == 0)
+    def _():
+        first = everyone[:, 0:8, :]
+        block = lax.broadcasted_iota(jnp.int32, first.shape, 1) % 2
+        variance = jnp.where(block == 0, everyone[:, 8:9, :], everyone[:, 9:10, :])
+        image = image_in[...] + variance * first
+        norm_now = row_gram(first, first)
+        step_size = row_solve(row_gram(first, image), norm_now)
+        residual = first - row_combine(image, row_weights(step_size))
+        norm_next = row_gram(residual, residual)
+        ratio = row_solve(norm_now, norm_next)
+        direction[...] = residual + row_combine(first, row_weights(ratio))
+        for k in range(SAMPLES):
+            for j in range(SAMPLES):
+                at = SAMPLES * k + j
+                sizes[at : at + 1] = step_size[k][j]
+                norm[at : at + 1] = norm_next[k][j]
+
+    spread_tiles(step, owners, direction, footprint, products, True)
+
+    @pl.when(step == pl.num_programs(0) - 1)
+    def _():
+        spread_end(products, second[...] == 1, lon, by_column, by_tile)
+
+
+def build_body(everyone, time_cov, lat_cov, tile_prior, time_part, row_part, hot, cols):
+    step = pl.program_id(0)
+    devices, tiles = everyone.shape[0], everyone.shape[2]
+    steps_here = time_part.shape[1]
+    rows = tile_prior.shape[0]
+
+    @pl.when(step == 0)
+    def _():
+        at = lax.broadcasted_iota(jnp.int32, (LAT, tiles), 0)
+        for d in range(devices):
+            place = everyone[d, 10:11, :].astype(jnp.int32)
+            here = slice(d * tiles, (d + 1) * tiles)
+            for kind, where, cov in (
+                (0, place // LAT + steps_here * d, time_cov),
+                (1, place % LAT, lat_cov),
+            ):
+                one = (at == where).astype(jnp.float32)
+                picked = jnp.dot(
+                    cov[...], one, precision=precise, preferred_element_type=jnp.float32
+                )
+                upper = picked.astype(jnp.bfloat16)
+                lower = (picked - upper.astype(jnp.float32)).astype(jnp.bfloat16)
+                cols[kind, 0:LAT, here] = upper
+                cols[kind, LAT : 2 * LAT, here] = lower
+                turned = one.T.astype(jnp.bfloat16)
+                hot[kind, here, 0:LAT] = turned
+                hot[kind, here, LAT : 2 * LAT] = turned
+                if kind == 0:
+                    for e in range(devices):
+                        mine = picked[e * steps_here : (e + 1) * steps_here]
+                        time_part[e, :, here] = mine
+                else:
+                    row_part[:, here] = picked
+
+    block = pl.ds(pl.multiple_of(step * rows, rows), rows)
+    by_time = jnp.dot(hot[0, block, :], cols[0], preferred_element_type=jnp.float32)
+    by_row = jnp.dot(hot[1, block, :], cols[1], preferred_element_type=jnp.float32)
+    tile_prior[...] = (by_time * by_row).astype(jnp.bfloat16)
+
+
+def mix_body(columns, tile_prior, mixed, total):
+    step = pl.program_id(0)
+    devices, width, tiles = columns.shape
+    part = tile_prior.shape[0] // tiles
+    lhs = jnp.concatenate([columns[step * part + p] for p in range(part)], axis=1)
+    product = jnp.dot(lhs, tile_prior[...], preferred_element_type=jnp.float32)
+
+    @pl.when(step == 0)
+    def _():
+        total[...] = product
+
+    @pl.when(step > 0)
+    def _():
+        total[...] += product
+
+    @pl.when(step == pl.num_programs(0) - 1)
+    def _():
+        for d in range(devices):
+            mixed[d] = total[:, d * tiles : (d + 1) * tiles].astype(jnp.bfloat16)
+
+
+def collect_body(owners, values, second, footprint, sums, rows):
+    step = pl.program_id(0)
+    chunks, slots = values.shape[0] // SAMPLES, footprint.shape[1]
+
+    @pl.when(step == 0)
+    def _():
+        is_second = second[...] == 1
+        for k in range(SAMPLES):
+            turned = values[k * chunks : (k + 1) * chunks].reshape(LON, -1)
+            turned = turned.astype(jnp.float32).T
+            rows[:, 2 * k, :] = jnp.where(is_second, 0.0, turned)
+            rows[:, 2 * k + 1, :] = jnp.where(is_second, turned, 0.0)
+
+    for q in range(owners):
+        owner = step * owners + q
+        total = 0.0
+        for c in range(slots):
+            total = total + lax.dot_general(
+                rows[owner * slots + c].astype(jnp.bfloat16),
+                footprint[q, c],
+                (((1,), (1,)), ((), ())),
+                preferred_element_type=jnp.float32,
+            )
+        sums[owner] = total
+
+
+def flux_body(
+    me, everyone, image_in, direction, sizes, norm, time_part, row_part,
+    gathered_one, gathered_two, answer, flux, total,
+):
+    step = pl.program_id(0)
+    steps = flux.shape[0]
+
+    @pl.when(step == 0)
+    def _():
+        second = direction[...]
+        block = lax.broadcasted_iota(jnp.int32, second.shape, 1) % 2
+        variance = jnp.where(block == 0, everyone[:, 8:9, :], everyone[:, 9:10, :])
+        image = image_in[...] + variance * second
+        grid = range(SAMPLES)
+        norm_now = [[norm[SAMPLES * k + j : SAMPLES * k + j + 1] for j in grid] for k in grid]
+        size_one = [[sizes[SAMPLES * k + j : SAMPLES * k + j + 1] for j in grid] for k in grid]
+        size_two = row_solve(row_gram(second, image), norm_now)
+        own = row_combine(everyone[me[0], 0:8, :], row_weights(size_one))
+        own = own + row_combine(direction[me[0]], row_weights(size_two))
+        for k in range(SAMPLES):
+            for b in range(2):
+                answer[b, k : k + 1, :] = own[2 * k + b : 2 * k + b + 1]
+        part = 256
+        for r in range(total.shape[0] // part):
+            at = slice(r * part, (r + 1) * part)
+            for j in range(SAMPLES):
+                value = 0.0
+                for gathered, size in ((gathered_one, size_one), (gathered_two, size_two)):
+                    for k in range(SAMPLES):
+                        piece = gathered[at, k * LON : (k + 1) * LON]
+                        value = value + piece.astype(jnp.float32) * size[k][j]
+                total[at, j * LON : (j + 1) * LON] = value.astype(jnp.bfloat16)
+
+    dense = []
+    for t in range(steps):
+        times = time_part[0, pl.ds(step * steps + t, 1), :]
+        dense.append((times * row_part[...]).astype(jnp.bfloat16))
+    result = jnp.dot(
+        jnp.concatenate(dense, axis=0), total[...], preferred_element_type=jnp.float32
+    )
+    for t in range(steps):
+        for k in range(SAMPLES):
+            flux[t, :, k, :] = result[t * LAT : (t + 1) * LAT, k * LON : (k + 1) * LON]
+
+
+def whole(shape):
+    return pl.BlockSpec(shape, lambda i, *_: (0,) * len(shape))
+
+
+def params():
+    return pltpu.CompilerParams(
+        dimension_semantics=("arbitrary",), vmem_limit_bytes=48 * 1024 * 1024
+    )
+
+
+def shape_of(shape, dtype):
+    return jax.ShapeDtypeStruct(shape, dtype)
+
+
+def cost(flops, moved):
+    return pl.CostEstimate(flops=flops, bytes_accessed=moved, transcendentals=0)
+
+
+def by_columns(
+    right_sides, obs_var, footprint, tile_block, tile_place, time_cov, lat_cov, lon_cov
+):
+    devices = lax.axis_size("tm")
+    me = lax.axis_index("tm")
+    owned = right_sides.shape[0]
+    steps_here = time_cov.shape[0] // devices
+    slots = tile_block.shape[1]
+    tiles = devices * slots
+    every_tile = devices * tiles
+    width = SAMPLES * LON // devices
+    f32, bf16 = jnp.float32, jnp.bfloat16
+
+    packed = jnp.concatenate(
+        [
+            right_sides.transpose(1, 0, 2).reshape(-1, 128),
+            obs_var,
+            tile_place.astype(f32).reshape(1, 128),
+            jnp.zeros((5, 128), f32),
+        ]
+    )
+    everyone = to_all(packed)
+    second = tile_block.reshape(tiles, 1)
+
+    stages = 4
+    owners = devices // stages
+    footprint_spec = pl.BlockSpec(
+        (owners, slots, BLOCK_OBS, LON), lambda i, *_: (i, 0, 0, 0)
+    )
+    everyone_spec = whole(everyone.shape)
+    vector_shape = (devices, 8, BLOCK_OBS)
+    vector_spec = whole(vector_shape)
+    second_spec, lon_spec = whole((tiles, 1)), whole((LON, LON))
+    column_shape, tile_shape = (devices, width, tiles), (tiles, SAMPLES * LON)
+    small_shape = (SAMPLES * SAMPLES, 128)
+    products = pltpu.VMEM((tiles, 8, LON), f32)
+    tile_flops = 2 * 8 * tiles * BLOCK_OBS * LON
+
+    by_column, by_tile = pl.pallas_call(
+        functools.partial(first_body, owners),
+        grid=(stages,),
+        in_specs=[everyone_spec, second_spec, lon_spec, footprint_spec],
+        out_specs=[whole(column_shape), whole(tile_shape)],
+        out_shape=[shape_of(column_shape, bf16), shape_of(tile_shape, bf16)],
+        scratch_shapes=[products],
+        compiler_params=params(),
+        cost_estimate=cost(tile_flops, footprint.size * 2),
+        name="spread_first",
+    )(everyone, second, lon_cov, footprint)
+    gathered_one = lax.all_gather(by_tile, "tm", axis=0, tiled=True)
+
+    build_stages = 8
+    build_rows = every_tile // build_stages
+    time_shape = (devices, steps_here, every_tile)
+    tile_prior, time_part, row_part = pl.pallas_call(
+        build_body,
+        grid=(build_stages,),
+        in_specs=[everyone_spec, whole((128, 128)), whole((128, 128))],
+        out_specs=[
+            pl.BlockSpec((build_rows, every_tile), lambda i: (i, 0)),
+            whole(time_shape),
+            whole((LAT, every_tile)),
+        ],
+        out_shape=[
+            shape_of((every_tile, every_tile), bf16),
+            shape_of(time_shape, f32),
+            shape_of((LAT, every_tile), f32),
+        ],
+        scratch_shapes=[
+            pltpu.VMEM((2, every_tile, 2 * LAT), bf16),
+            pltpu.VMEM((2, 2 * LAT, every_tile), bf16),
+        ],
+        compiler_params=params(),
+        cost_estimate=cost(4 * every_tile * every_tile * 256, every_tile * every_tile * 2),
+        name="build_prior",
+    )(everyone, time_cov, lat_cov)
+
+    def prior(columns):
+        sent = lax.all_to_all(columns, "tm", split_axis=0, concat_axis=0, tiled=True)
+        mix_stages = 4
+        mixed = pl.pallas_call(
+            mix_body,
+            grid=(mix_stages,),
+            in_specs=[
+                whole(column_shape),
+                pl.BlockSpec((every_tile // mix_stages, every_tile), lambda i: (i, 0)),
+            ],
+            out_specs=whole(column_shape),
+            out_shape=shape_of(column_shape, bf16),
+            scratch_shapes=[pltpu.VMEM((width, every_tile), f32)],
+            compiler_params=params(),
+            cost_estimate=cost(2 * width * every_tile**2, every_tile**2 * 2),
+            name="mix_columns",
+        )(sent, tile_prior)
+        return lax.all_to_all(mixed, "tm", split_axis=0, concat_axis=0, tiled=True)
+
+    def collect(values):
+        sums = pl.pallas_call(
+            functools.partial(collect_body, owners),
+            grid=(stages,),
+            in_specs=[whole(column_shape), second_spec, footprint_spec],
+            out_specs=vector_spec,
+            out_shape=shape_of(vector_shape, f32),
+            scratch_shapes=[products],
+            compiler_params=params(),
+            cost_estimate=cost(tile_flops, footprint.size * 2),
+            name="collect",
+        )(values, second, footprint)
+        terms = lax.all_to_all(sums, "tm", split_axis=0, concat_axis=0, tiled=True)
+        return to_all(terms.sum(0))
+
+    image = collect(prior(by_column))
+    by_column, by_tile, direction, sizes, norm = pl.pallas_call(
+        functools.partial(update_body, owners),
+        grid=(stages,),
+        in_specs=[everyone_spec, vector_spec, second_spec, lon_spec, footprint_spec],
+        out_specs=[
+            whole(column_shape),
+            whole(tile_shape),
+            vector_spec,
+            whole(small_shape),
+            whole(small_shape),
+        ],
+        out_shape=[
+            shape_of(column_shape, bf16),
+            shape_of(tile_shape, bf16),
+            shape_of(vector_shape, f32),
+            shape_of(small_shape, f32),
+            shape_of(small_shape, f32),
+        ],
+        scratch_shapes=[products],
+        compiler_params=params(),
+        cost_estimate=cost(tile_flops, footprint.size * 2),
+        name="update_spread",
+    )(everyone, image, second, lon_cov, footprint)
+    gathered_two = lax.all_gather(by_tile, "tm", axis=0, tiled=True)
+
+    image = collect(prior(by_column))
+    flux_stages = 4
+    flux_steps = steps_here // flux_stages
+    answer, flux = pl.pallas_call(
+        flux_body,
+        grid_spec=pltpu.PrefetchScalarGridSpec(
+            num_scalar_prefetch=1,
+            grid=(flux_stages,),
+            in_specs=[
+                everyone_spec,
+                vector_spec,
+                vector_spec,
+                whole(small_shape),
+                whole(small_shape),
+                pl.BlockSpec((1, steps_here, every_tile), lambda i, me: (me[0], 0, 0)),
+                whole((LAT, every_tile)),
+                whole((every_tile, SAMPLES * LON)),
+                whole((every_tile, SAMPLES * LON)),
+            ],
+            out_specs=[
+                whole((owned, SAMPLES, BLOCK_OBS)),
+                pl.BlockSpec((flux_steps, LAT, SAMPLES, LON), lambda i, me: (i, 0, 0, 0)),
+            ],
+            scratch_shapes=[pltpu.VMEM((every_tile, SAMPLES * LON), bf16)],
+        ),
+        out_shape=[
+            shape_of((owned, SAMPLES, BLOCK_OBS), f32),
+            shape_of((steps_here, LAT, SAMPLES, LON), f32),
+        ],
+        compiler_params=params(),
+        cost_estimate=cost(2 * steps_here * LAT * every_tile * SAMPLES * LON, 8 << 20),
+        name="update_flux",
+    )(
+        me.reshape(1).astype(jnp.int32), everyone, image, direction, sizes, norm,
+        time_part, row_part, gathered_one, gathered_two,
+    )
+    return (answer, flux)
+
+
+def local(right_sides, obs_var, footprint, tile_block, tile_place, *covariances):
+    devices = lax.axis_size("tm")
+    tiles = tile_block.size
+    fits = devices * tiles <= 2048 and devices % 4 == 0 and tiles == 128
+    fits = fits and right_sides.shape[0] == 2 and (SAMPLES * LON) % (32 * devices) == 0
+    fits = fits and (covariances[0].shape[0] // devices) % 4 == 0
+    plan = by_columns if fits else by_gather
+    return plan(right_sides, obs_var, footprint, tile_block, tile_place, *covariances)
+
+
 def solution(mesh):
     in_specs = (
         P(("grp", "tm"), None, None),

time: 205 us -> 166 us (0.81)
  waiting for transfers between devices: 90.1 us -> 13.8 us
  blocking collectives: 0 us -> 67.9 us
  matrix products: 43.4 us -> 0 us
  Pallas kernels: 0 us -> 43.4 us
  local copies, waits for them, and re-layouts: 21.7 us -> 9.91 us
  other arithmetic: 12.2 us -> 1.48 us
  starting transfers between devices: 22.2 us -> 14.7 us
    all_to_all x0 -> x6, blocking collectives: none -> 67.9 us  [the longest x2 27 us: prior(): return lax.all_to_all(mixed, 'tm', split_axis=0, concat_axis=0, tiled=True)]
    all_gather x2, waiting for transfers between devices: 65.3 us -> 0.01 us  [the longest x1 0.01 us: by_columns(): gathered_one = lax.all_gather(by_tile, 'tm', axis=0, tiled=True)]
    pallas_call x0 -> x8, Pallas kernels: none -> 43.4 us  [the longest x2 10.6 us: prior(): pl.pallas_call(mix_body, grid=(mix_stages,), in_specs=[whole(column_shape...]
    dot_general x24 -> x0, matrix products: 42.2 us -> none  [the longest x2 10.6 us: mix(): return jnp.einsum('tkl,kj->tjl', whole, size, precision=precise)]
    all_to_all x2 -> x1, waiting for transfers between devices: 8.18 us -> 0.01 us  [prior(): lax.all_to_all(columns, 'tm', split_axis=0, concat_axis=0, tiled=True)]
    another operation x15 -> x0, other arithmetic: 6.2 us -> none  [the longest x9 3.23 us: solve_spd(): factor = jnp.linalg.cholesky(matrix)]
    reshape x9 -> x2, local copies, waits for them, and re-layouts: 6.16 us -> 0.16 us  [the longest x1 0.09 us: by_columns(): tile_place.astype(f32).reshape(1, 128)]
    gather x3 -> x0, local copies, waits for them, and re-layouts: 5.66 us -> none  [the longest x1 4.17 us: local(): mine = jnp.take(dense, tile_place.reshape(-1), axis=0)]
  transfers between devices with their start and end apart: 7 -> 5, of which waited for: 7 -> 2; matrix products, arithmetic and copies ran while one was open for 11% -> 1% of each run, Pallas kernels for 0% -> 18%
where the time goes in v2:
time: 166 us; the launch traced here: 165 us
  blocking collectives  67.9 us (41%)
  Pallas kernels  43.4 us (26%)
  starting transfers between devices  14.7 us (9%)
  between operations  14.1 us (8%)
  waiting for transfers between devices  13.8 us (8%)
  local copies, waits for them, and re-layouts  9.91 us (6%)
    all_to_all x2, blocking collectives, prior(): return lax.all_to_all(mixed, 'tm', split_axis=0, concat_axis=0, tiled=True)  27 us
    all_to_all x2, blocking collectives, collect(): terms = lax.all_to_all(sums, 'tm', split_axis=0, concat_axis=0, tiled=True)  20.9 us
    all_to_all x2, waiting for transfers between devices, to_all(): return lax.all_to_all(copies, 'tm', split_axis=0, concat_axis=0, tiled=True)  13.7 us
    all_to_all x2, starting transfers between devices, to_all(): return lax.all_to_all(copies, 'tm', split_axis=0, concat_axis=0, tiled=True)  11.1 us
    pallas_call x2, Pallas kernels, prior(): pl.pallas_call(mix_body, grid=(mix_stages,), in_specs=[whole(column_shape...  10.6 us
    all_to_all x1, blocking collectives, prior(): lax.all_to_all(columns, 'tm', split_axis=0, concat_axis=0, tiled=True)  10.5 us
    pallas_call x1, Pallas kernels, by_columns(): pl.pallas_call(flux_body, grid_spec=pltpu.PrefetchScalarGridSpec(num_scal...  10.4 us
    pallas_call x1, Pallas kernels, by_columns(): pl.pallas_call(build_body, grid=(build_stages,), in_specs=[everyone_spec,...  10.3 us
  transfers between devices with their start and end apart: 5, of which 2 were waited for; matrix products, arithmetic and copies ran while one was open for 1% of the time, Pallas kernels for 18%

profile of v2, /device:TPU:0, one launch (start us, length us, event | category | flops | bytes accessed | tf_op | source)
XLA Modules:
  0.0 165.3 jit_solution(13318422402480689301)
XLA Ops:
  7.2 0.7 convert_element_type.3
  7.9 0.1 copy.17
  7.9 0.1 reshape.21
  8.0 0.7 copy.16
  8.7 0.1 pad.3.clone
  8.8 0.8 maximum_maximum_fusion
  9.5 0.7 broadcast_in_dim.9
  10.2 7.4 %all-to-all-start = ((f32[16,16,128]{2,1,0:T(8,128)}), f32[16,16,128]{2,1,0:T(8,128)S(1)}, u32[]{:S(2)}, u32[]{:S(2)}) async-start(f32[16,16,128]{2,1,0:T(8,128)} %broadcast_in_dim.9), calls=%async_computation | async-start | bytes 262144 | tf_op jit(solution)/shard_map/all_to_all | solution.py:39
  17.6 0.0 all-gather.3.cloned.1.call-start
  17.6 0.8 copy.18
  18.4 0.1 reshape.23.second
  18.5 7.0 %all-to-all-done.everyone = f32[16,16,128]{2,1,0:T(8,128)S(1)} async-done(((f32[16,16,128]{2,1,0:T(8,128)}), f32[16,16,128]{2,1,0:T(8,128)S(1)}, u32[]{:S(2)}, u32[]{:S(2)}) %all-to-all-start) | async-done | bytes 131104 | tf_op jit(solution)/shard_map/all_to_all | solution.py:39
  25.5 0.0 copy-start
  25.5 2.2 %copy-done = bf16[16,8,128,128]{3,2,1,0:T(8,128)(2,1)S(1)} copy-done((bf16[16,8,128,128]{3,2,1,0:T(8,128)(2,1)S(1)}, bf16[16,8,128,128]{3,2,1,0:T(8,128)(2,1)}, u32[]{:S(2)}) %copy-start) | copy-done | bytes 4194328
  27.7 0.0 copy-start.4
  27.7 0.8 copy-done.4
  28.6 0.0 copy-start.7
  28.6 0.0 copy-start.8
  28.6 2.9 %spread_first.1 = (bf16[16,32,128]{2,1,0:T(8,128)(2,1)}, bf16[128,512]{1,0:T(8,128)(2,1)}) custom-call(f32[16,16,128]{2,1,0:T(8,128)S(1)} %all-to-all-done.everyone, s32[128,1]{1,0:T(8,128)S(1)} %reshape.23.second, f32[128,128]{1,0:T(8,128)S(1)} %copy-done.4, bf16[16,8,128,128]{3,2,1,0:T(8,128)(2,1)S(1)} %copy-done), custom_call_target="tpu_custom_call" | custom-call | flops 33554432 | bytes 4194304 | tf_op jit(solution)/shard_map/spread_first/pallas_call | solution.py:461
  31.5 0.0 all-gather.3.cloned.1.call-update
  31.5 3.5 %all-to-all-start.1 = ((bf16[16,32,128]{2,1,0:T(8,128)(2,1)}), bf16[16,32,128]{2,1,0:T(8,128)(2,1)S(1)}, u32[]{:S(2)}, u32[]{:S(2)}) async-start(bf16[16,32,128]{2,1,0:T(8,128)(2,1)} %get-tuple-element.12), calls=%async_computation.1 | async-start | bytes 262144 | tf_op jit(solution)/shard_map/all_to_all | solution.py:501
  35.0 0.0 all-gather.5.cloned.1.call-start
  35.1 0.0 copy-done.7
  35.1 0.0 copy-done.8
  35.1 10.3 %build_prior.1 = (bf16[2048,2048]{1,0:T(8,128)(2,1)}, f32[16,8,2048]{2,1,0:T(8,128)S(1)}, f32[128,2048]{1,0:T(8,128)S(1)}) custom-call(f32[16,16,128]{2,1,0:T(8,128)S(1)} %all-to-all-done.everyone, f32[128,128]{1,0:T(8,128)S(1)} %copy-done.7, f32[128,128]{1,0:T(8,128)S(1)} %copy-done.8), custom_call_target="tpu_custom_call" | custom-call | flops 4294967296 | bytes 8388608 | tf_op jit(solution)/shard_map/build_prior/pallas_call | solution.py:477
  45.5 0.0 all-to-all-done.1.columns
  45.5 0.0 copy-start.1
  45.5 5.3 %mix_columns.2 = bf16[16,32,128]{2,1,0:T(8,128)(2,1)S(1)} custom-call(bf16[16,32,128]{2,1,0:T(8,128)(2,1)S(1)} %all-to-all-done.1.columns, bf16[2048,2048]{1,0:T(8,128)(2,1)} %get-tuple-element.13.tile_prior), custom_call_target="tpu_custom_call" | custom-call | flops 268435456 | bytes 8388608 | tf_op jit(solution)/shard_map/mix_columns/pallas_call | solution.py:503
  50.8 15.8 %all_to_all.45.values = bf16[16,32,128]{2,1,0:T(8,128)(2,1)S(1)} all-to-all(bf16[16,32,128]{2,1,0:T(8,128)(2,1)S(1)} %mix_columns.2), channel_id=1, replica_groups=mesh['grp'=2,'tm'=16] {'tm'}, dimensions={0} | all-to-all | bytes 262144 | tf_op jit(solution)/shard_map/all_to_all | solution.py:517
  66.6 0.0 copy-done.1
  66.6 0.0 copy-start.5
  66.6 3.0 %collect.2 = f32[16,8,128]{2,1,0:T(8,128)S(1)} custom-call(bf16[16,32,128]{2,1,0:T(8,128)(2,1)S(1)} %all_to_all.45.values, s32[128,1]{1,0:T(8,128)S(1)} %reshape.23.second, bf16[16,8,128,128]{3,2,1,0:T(8,128)(2,1)S(1)} %copy-done.1), custom_call_target="tpu_custom_call" | custom-call | flops 33554432 | bytes 4194304 | tf_op jit(solution)/shard_map/collect/pallas_call | solution.py:520
  69.6 9.5 %all_to_all.46 = f32[16,8,128]{2,1,0:T(8,128)S(1)} all-to-all(f32[16,8,128]{2,1,0:T(8,128)S(1)} %collect.2), channel_id=1, replica_groups=mesh['grp'=2,'tm'=16] {'tm'}, dimensions={0} | all-to-all | bytes 131072 | tf_op jit(solution)/shard_map/all_to_all | solution.py:531
  79.1 9.5 %all_to_all.47.image_in = f32[16,8,128]{2,1,0:T(8,128)S(1)} all-to-all(f32[16,8,128]{2,1,0:T(8,128)S(1)} %broadcast_in_dim.10), channel_id=1, replica_groups=mesh['grp'=2,'tm'=16] {'tm'}, dimensions={0} | all-to-all | bytes 131072 | tf_op jit(solution)/shard_map/all_to_all | solution.py:39
  88.6 0.0 copy-done.5
  88.6 0.0 copy-start.2
  88.6 2.2 %copy-done.2 = bf16[16,8,128,128]{3,2,1,0:T(8,128)(2,1)S(1)} copy-done((bf16[16,8,128,128]{3,2,1,0:T(8,128)(2,1)S(1)}, bf16[16,8,128,128]{3,2,1,0:T(8,128)(2,1)}, u32[]{:S(2)}) %copy-start.2) | copy-done | bytes 4194328
  90.8 3.2 %update_spread.1 = (bf16[16,32,128]{2,1,0:T(8,128)(2,1)S(1)}, bf16[128,512]{1,0:T(8,128)(2,1)}, f32[16,8,128]{2,1,0:T(8,128)S(1)}, f32[16,128]{1,0:T(8,128)S(1)}, f32[16,128]{1,0:T(8,128)S(1)}) custom-call(f32[16,16,128]{2,1,0:T(8,128)S(1)} %all-to-all-done.everyone, f32[16,8,128]{2,1,0:T(8,128)S(1)} %all_to_all.47.image_in, s32[128,1]{1,0:T(8,128)S(1)} %reshape.23.second, ...), custom_call_target="tpu_custom_call" | custom-call | flops 33554432 | bytes 4194304 | tf_op jit(solution)/shard_map/update_spread/pallas_call | solution.py:535
  94.0 0.0 all-gather.5.cloned.1.call-update
  94.0 10.5 %all_to_all.48.columns = bf16[16,32,128]{2,1,0:T(8,128)(2,1)S(1)} all-to-all(bf16[16,32,128]{2,1,0:T(8,128)(2,1)S(1)} %get-tuple-element.14), channel_id=1, replica_groups=mesh['grp'=2,'tm'=16] {'tm'}, dimensions={0} | all-to-all | bytes 262144 | tf_op jit(solution)/shard_map/all_to_all | solution.py:501
  104.5 0.0 copy-start.3
  104.6 5.3 %mix_columns.3 = bf16[16,32,128]{2,1,0:T(8,128)(2,1)S(1)} custom-call(bf16[16,32,128]{2,1,0:T(8,128)(2,1)S(1)} %all_to_all.48.columns, bf16[2048,2048]{1,0:T(8,128)(2,1)} %get-tuple-element.13.tile_prior), custom_call_target="tpu_custom_call" | custom-call | flops 268435456 | bytes 8388608 | tf_op jit(solution)/shard_map/mix_columns/pallas_call | solution.py:503
  109.9 11.2 %all_to_all.49.values = bf16[16,32,128]{2,1,0:T(8,128)(2,1)S(1)} all-to-all(bf16[16,32,128]{2,1,0:T(8,128)(2,1)S(1)} %mix_columns.3), channel_id=1, replica_groups=mesh['grp'=2,'tm'=16] {'tm'}, dimensions={0} | all-to-all | bytes 262144 | tf_op jit(solution)/shard_map/all_to_all | solution.py:517
  121.1 0.0 copy-done.3
  121.1 3.0 %collect.3 = f32[16,8,128]{2,1,0:T(8,128)S(1)} custom-call(bf16[16,32,128]{2,1,0:T(8,128)(2,1)S(1)} %all_to_all.49.values, s32[128,1]{1,0:T(8,128)S(1)} %reshape.23.second, bf16[16,8,128,128]{3,2,1,0:T(8,128)(2,1)S(1)} %copy-done.3), custom_call_target="tpu_custom_call" | custom-call | flops 33554432 | bytes 4194304 | tf_op jit(solution)/shard_map/collect/pallas_call | solution.py:520
  124.1 11.4 %all_to_all.50 = f32[16,8,128]{2,1,0:T(8,128)S(1)} all-to-all(f32[16,8,128]{2,1,0:T(8,128)S(1)} %collect.3), channel_id=1, replica_groups=mesh['grp'=2,'tm'=16] {'tm'}, dimensions={0} | all-to-all | bytes 131072 | tf_op jit(solution)/shard_map/all_to_all | solution.py:531
  135.5 0.6 broadcast_in_dim.11
  136.1 3.7 %all-to-all-start.8 = ((f32[16,8,128]{2,1,0:T(8,128)}), f32[16,8,128]{2,1,0:T(8,128)S(1)}, u32[]{:S(2)}, u32[]{:S(2)}) async-start(f32[16,8,128]{2,1,0:T(8,128)} %broadcast_in_dim.11), calls=%async_computation.8 | async-start | bytes 131072 | tf_op jit(solution)/shard_map/all_to_all | solution.py:39
  139.8 6.7 %all-to-all-done.8.image_in = f32[16,8,128]{2,1,0:T(8,128)S(1)} async-done(((f32[16,8,128]{2,1,0:T(8,128)}), f32[16,8,128]{2,1,0:T(8,128)S(1)}, u32[]{:S(2)}, u32[]{:S(2)}) %all-to-all-start.8) | async-done | bytes 65568 | tf_op jit(solution)/shard_map/all_to_all | solution.py:39
  146.5 0.0 all-gather.3.cloned.1.call-done.gathered_one
  146.5 0.0 all-gather.5.cloned.1.call-done.gathered_two
  146.5 0.0 copy-start.6
  146.5 1.6 copy-done.6
  148.1 10.4 %update_flux.1 = (f32[2,4,128]{2,1,0:T(4,128)}, f32[8,128,4,128]{3,2,1,0:T(4,128)}) custom-call(s32[1]{0:T(128)} %bitcast.me, f32[16,16,128]{2,1,0:T(8,128)S(1)} %all-to-all-done.everyone, f32[16,8,128]{2,1,0:T(8,128)S(1)} %all-to-all-done.8.image_in, f32[16,8,128]{2,1,0:T(8,128)S(1)} %get-tuple-element.15.direction, f32[16,128]{1,0:T(8,128)S(1)} %get-tuple-element.16.sizes, ...), custom_call_target="tpu_custom_call" | custom-call | flops 2147483648 | bytes 8388608 | tf_op jit(solution)/shard_map/update_flux/pallas_call | solution.py:563
  (4 shorter events, 0.0 us)
Async XLA Ops:
  10.2 15.3 %all-to-all-start = ((f32[16,16,128]{2,1,0:T(8,128)}), f32[16,16,128]{2,1,0:T(8,128)S(1)}, u32[]{:S(2)}, u32[]{:S(2)}) async-start(f32[16,16,128]{2,1,0:T(8,128)} %broadcast_in_dim.9), calls=%async_computation | async-start | bytes 262144 | tf_op jit(solution)/shard_map/all_to_all | solution.py:39
  17.6 128.9 %all-gather.3.cloned.1.call-start = ((), (), s32[]{:S(2)}) async-start(), calls=%async_computation.9 | async-start | bytes 2228224 | tf_op jit(solution)/shard_map/all_gather | solution.py:472
  25.5 2.2 %copy-start = (bf16[16,8,128,128]{3,2,1,0:T(8,128)(2,1)S(1)}, bf16[16,8,128,128]{3,2,1,0:T(8,128)(2,1)}, u32[]{:S(2)}) copy-start(bf16[16,8,128,128]{3,2,1,0:T(8,128)(2,1)} %footprint.7) | copy-start | bytes 12582916
  27.7 0.8 copy-start.4
  28.6 6.5 %copy-start.7 = (f32[128,128]{1,0:T(8,128)S(1)}, f32[128,128]{1,0:T(8,128)}, u32[]{:S(2)}) copy-start(f32[128,128]{1,0:T(8,128)} %time_cov.1) | copy-start | bytes 196612
  28.6 6.5 %copy-start.8 = (f32[128,128]{1,0:T(8,128)S(1)}, f32[128,128]{1,0:T(8,128)}, u32[]{:S(2)}) copy-start(f32[128,128]{1,0:T(8,128)} %lat_cov.1) | copy-start | bytes 196612
  31.5 13.9 %all-to-all-start.1 = ((bf16[16,32,128]{2,1,0:T(8,128)(2,1)}), bf16[16,32,128]{2,1,0:T(8,128)(2,1)S(1)}, u32[]{:S(2)}, u32[]{:S(2)}) async-start(bf16[16,32,128]{2,1,0:T(8,128)(2,1)} %get-tuple-element.12), calls=%async_computation.1 | async-start | bytes 262144 | tf_op jit(solution)/shard_map/all_to_all | solution.py:501
  35.0 111.4 %all-gather.5.cloned.1.call-start = ((), (), s32[]{:S(2)}) async-start(), calls=%async_computation.10 | async-start | bytes 2228224 | tf_op jit(solution)/shard_map/all_gather | solution.py:558
  45.5 21.1 %copy-start.1 = (bf16[16,8,128,128]{3,2,1,0:T(8,128)(2,1)S(1)}, bf16[16,8,128,128]{3,2,1,0:T(8,128)(2,1)}, u32[]{:S(2)}) copy-start(bf16[16,8,128,128]{3,2,1,0:T(8,128)(2,1)} %footprint.7) | copy-start | bytes 12582916
  66.6 22.0 %copy-start.5 = (f32[128,128]{1,0:T(8,128)S(1)}, f32[128,128]{1,0:T(8,128)}, u32[]{:S(2)}) copy-start(f32[128,128]{1,0:T(8,128)} %lon.3) | copy-start | bytes 196612
  88.6 2.2 %copy-start.2 = (bf16[16,8,128,128]{3,2,1,0:T(8,128)(2,1)S(1)}, bf16[16,8,128,128]{3,2,1,0:T(8,128)(2,1)}, u32[]{:S(2)}) copy-start(bf16[16,8,128,128]{3,2,1,0:T(8,128)(2,1)} %footprint.7) | copy-start | bytes 12582916
  104.5 16.6 %copy-start.3 = (bf16[16,8,128,128]{3,2,1,0:T(8,128)(2,1)S(1)}, bf16[16,8,128,128]{3,2,1,0:T(8,128)(2,1)}, u32[]{:S(2)}) copy-start(bf16[16,8,128,128]{3,2,1,0:T(8,128)(2,1)} %footprint.7) | copy-start | bytes 12582916
  136.1 10.4 %all-to-all-start.8 = ((f32[16,8,128]{2,1,0:T(8,128)}), f32[16,8,128]{2,1,0:T(8,128)S(1)}, u32[]{:S(2)}, u32[]{:S(2)}) async-start(f32[16,8,128]{2,1,0:T(8,128)} %broadcast_in_dim.11), calls=%async_computation.8 | async-start | bytes 131072 | tf_op jit(solution)/shard_map/all_to_all | solution.py:39
  146.5 1.6 copy-start.6
Sparse Core Ops, SparseCore 0:
  31.6 40.5 all-gather.2
  94.1 38.7 all-gather.4
